TPU v7x, 32 devices: a whole 2x2x4 slice. The times are simulated.
32 devices in a mesh: ta: 4 (over z), ha: 2 (over y), wa: 4 (over x, core).
Axes of the slice: x: 2, y: 2, z: 4, core: 2. Of those that a mesh axis runs over, the one named last changes fastest.
Arguments:
- stream: bfloat16 [4, 2, 384, 1536], P('ta', 'ha'), may hold values from -40 to 40
- queries: bfloat16 [4, 2, 384, 1536], P('ta', 'ha', None, 'wa'), may hold values from -6 to 6
- key_heads: bfloat16 [4, 2, 384, 1536], P('ta', 'ha', None, 'wa'), may hold values from -6 to 6
- value_heads: bfloat16 [4, 2, 384, 1536], P('ta', 'ha', None, 'wa'), may hold values from -6 to 6
- out_weight: bfloat16 [1536, 1536], P('wa'), may hold values from -0.15625 to 0.15625
- norm_gain: float32 [1536], replicated, may hold values from 0.25 to 1.75
- up_weight: bfloat16 [1536, 6144], P(('ta', 'ha'), 'wa'), may hold values from -0.15625 to 0.15625
- down_weight: bfloat16 [6144, 1536], P('wa', ('ta', 'ha')), may hold values from -0.078125 to 0.078125
- tile_route: int32 [4, 2, 1], P('ta', 'ha'), may hold values 0 or 1
- cotangent: bfloat16 [4, 2, 384, 1536], P('ta', 'ha'), may hold values from -6 to 6
Outputs:
- stream_grad: bfloat16 [4, 2, 384, 1536], P('ta', 'ha')
- query_grad: bfloat16 [4, 2, 384, 1536], P('ta', 'ha', None, 'wa')
- key_grad: bfloat16 [4, 2, 384, 1536], P('ta', 'ha', None, 'wa')
- value_grad: bfloat16 [4, 2, 384, 1536], P('ta', 'ha', None, 'wa')
- out_weight_grad: float32 [1536, 1536], P('wa', ('ta', 'ha'))
All inputs are finite; a program needn't handle non-finite values. No bound on the sum of `tile_route` on one device may be relied on, other than what follows from the above.
Results may differ from a plain program's by a relative error of at most 0.014.
Values may be sent and summed in bfloat16 or wider, within the bound.
A program may use at most 128 MiB of HBM per device.

v0:
```python
import math
import jax
import jax.numpy as jnp
from jax import lax
from jax.sharding import PartitionSpec as P

HS = 128
TILE = 384
EPSILON = 1e-06
TANH_SCALE = 0.7978845608028654
CUBIC_COEF = 0.044715
NEG_FILL = -1e30


def extended(cells, sides, width):
    for axis, dim in sides:
        count = lax.axis_size(axis)
        ends = count - 1
        head = lax.slice_in_dim(cells, 0, width, axis=dim)
        tail = lax.slice_in_dim(cells, cells.shape[dim] - width, cells.shape[dim], axis=dim)
        cells = jnp.concatenate(
            [
                lax.ppermute(tail, axis, [(i, (i + 1) % count) for i in range(ends)]),
                cells,
                lax.ppermute(head, axis, [((i + 1) % count, i) for i in range(ends)]),
            ],
            axis=dim,
        )
    return cells


def from_behind(array, axis, by):
    devices = lax.axis_size(axis)
    pairs = [(i, i + by) for i in range(devices) if 0 <= i + by < devices]
    return lax.ppermute(array, axis, pairs)


def gelu_slope(pre_act):
    tanh_arg = TANH_SCALE * (pre_act + CUBIC_COEF * pre_act * pre_act * pre_act)
    tanh_val = jnp.tanh(tanh_arg)
    return 0.5 * (1.0 + tanh_val) + 0.5 * pre_act * (1.0 - tanh_val * tanh_val) * TANH_SCALE * (
        1.0 + 3.0 * CUBIC_COEF * pre_act * pre_act
    )


def head_probs(query_rows, key_rows, key_marks, score_scale):
    scores = (
        jnp.einsum("qd,kd->qk", query_rows, key_rows, preferred_element_type=jnp.float32)
        * score_scale
    )
    scores = jnp.where(key_marks[None, :] > 0.5, scores, NEG_FILL)
    row_max = jnp.max(scores, axis=1)
    weights = jnp.exp(scores - row_max[:, None])
    row_total = jnp.sum(weights, axis=1)
    return (weights / row_total[:, None], row_max, row_total)


def layer_norm(residual):
    mean_val = jnp.mean(residual, axis=1, keepdims=True)
    centered = residual - mean_val
    variance = jnp.mean(centered * centered, axis=1, keepdims=True)
    inv_std = lax.rsqrt(variance + EPSILON)
    return (centered * inv_std, inv_std)


def norm_backward(norm_grad, norm_gain, normed, inv_std):
    scaled = norm_grad * norm_gain
    return (
        scaled
        - jnp.mean(scaled, axis=1, keepdims=True)
        - normed * jnp.mean(scaled * normed, axis=1, keepdims=True)
    ) * inv_std


def shards(
    stream,
    queries,
    key_heads,
    value_heads,
    out_weight,
    norm_gain,
    up_weight,
    down_weight,
    tile_route,
    cotangent,
):
    row_count = stream.shape[2]
    model_width = stream.shape[3]
    channels = queries.shape[3]
    heads_here = channels // HS
    tile_count = row_count // TILE
    score_scale = 1.0 / math.sqrt(HS)
    tile_ids = jnp.arange(tile_count, dtype=jnp.int32)
    tile_marks = tile_route.astype(jnp.bfloat16)
    faces_key, faces_value, faces_marks = (
        extended(key_heads, (("ta", 0), ("ha", 1)), 1),
        extended(value_heads, (("ta", 0), ("ha", 1)), 1),
        extended(tile_marks, (("ta", 0), ("ha", 1)), 1),
    )

    def window():
        key_block = faces_key.reshape(9 * TILE, heads_here, HS)
        value_block = faces_value.reshape(9 * TILE, heads_here, HS)
        mark_block = faces_marks.reshape(9).astype(jnp.float32)
        key_marks = jnp.repeat(mark_block, TILE)
        query_tile = queries.reshape(TILE, heads_here, HS)
        return (
            query_tile.transpose(1, 0, 2),
            key_block.transpose(1, 0, 2),
            value_block.transpose(1, 0, 2),
            key_marks,
        )

    def forward_tile(tile_index):
        own_mark = tile_marks[0, 0, tile_index]
        query_tile, key_block, value_block, key_marks = window()

        def per_head(operands):
            query_rows, key_rows, value_rows = operands
            weights, row_max, row_total = head_probs(query_rows, key_rows, key_marks, score_scale)
            mixture = jnp.dot(
                weights.astype(jnp.bfloat16), value_rows, preferred_element_type=jnp.float32
            )
            return (mixture, row_max, row_total)

        mixture, row_max, row_total = lax.map(per_head, (query_tile, key_block, value_block))
        scaled = (mixture * own_mark.astype(jnp.float32)).astype(jnp.bfloat16)
        return (scaled.transpose(1, 0, 2).reshape(TILE, channels), row_max, row_total)

    attn_tiles, max_tiles, total_tiles = lax.map(forward_tile, tile_ids)
    attention = attn_tiles.reshape(row_count, channels)
    attn_part = jnp.dot(attention, out_weight, preferred_element_type=jnp.float32)
    head_share = lax.psum_scatter(attn_part, "wa", scatter_dimension=0, tiled=True)
    share_rows = head_share.shape[0]
    share_start = lax.axis_index("wa") * share_rows
    flat_stream = stream.reshape(row_count, model_width)
    flat_cot = cotangent.reshape(row_count, model_width)
    residual = (
        lax.dynamic_slice_in_dim(flat_stream, share_start, share_rows, 0).astype(jnp.float32)
        + head_share
    )
    normed, inv_std = layer_norm(residual)
    hidden_share = (normed * norm_gain).astype(jnp.bfloat16)
    hidden_in = lax.all_gather(hidden_share, "wa", axis=0, tiled=True)
    up_full, down_full = (
        lax.all_gather(up_weight, ("ta", "ha"), axis=0, tiled=True),
        lax.all_gather(down_weight, ("ta", "ha"), axis=1, tiled=True),
    )
    pre_act = jnp.dot(hidden_in, up_full, preferred_element_type=jnp.float32)
    act_grad = jnp.einsum("td,fd->tf", flat_cot, down_full, preferred_element_type=jnp.float32)
    pre_grad = (act_grad * gelu_slope(pre_act)).astype(jnp.bfloat16)
    norm_part = jnp.einsum("tf,df->td", pre_grad, up_full, preferred_element_type=jnp.float32)
    norm_share = lax.psum_scatter(norm_part, "wa", scatter_dimension=0, tiled=True)
    cot_share = lax.dynamic_slice_in_dim(flat_cot, share_start, share_rows, 0).astype(jnp.float32)
    grad_share = (cot_share + norm_backward(norm_share, norm_gain, normed, inv_std)).astype(
        jnp.bfloat16
    )
    stream_grad = lax.all_gather(grad_share, "wa", axis=0, tiled=True)
    weight_part = jnp.einsum(
        "tc,td->cd", attention, stream_grad, preferred_element_type=jnp.float32
    )
    out_weight_grad = lax.psum_scatter(weight_part, ("ta", "ha"), scatter_dimension=1, tiled=True)
    attn_grad = jnp.einsum(
        "td,cd->tc", stream_grad, out_weight, preferred_element_type=jnp.float32
    ).astype(jnp.bfloat16)
    row_marks = jnp.repeat(tile_marks.reshape(tile_count), TILE)
    masked_grad = attn_grad * row_marks[:, None]

    def own_side():
        query_tile, key_block, value_block, key_marks = window()
        grad_tile = masked_grad.reshape(TILE, heads_here, HS).transpose(1, 0, 2)

        def head_back(operands):
            query_rows, key_rows, value_rows, grad_rows = operands
            weights = head_probs(query_rows, key_rows, key_marks, score_scale)[0]
            grad_probs = jnp.einsum(
                "qd,kd->qk", grad_rows, value_rows, preferred_element_type=jnp.float32
            )
            row_delta = jnp.sum(weights * grad_probs, axis=1)
            grad_scores = (weights * (grad_probs - row_delta[:, None]) * score_scale).astype(
                jnp.bfloat16
            )
            query_part = jnp.dot(grad_scores, key_rows, preferred_element_type=jnp.float32).astype(
                jnp.bfloat16
            )
            value_part = jnp.einsum(
                "qk,qd->kd",
                weights.astype(jnp.bfloat16),
                grad_rows,
                preferred_element_type=jnp.float32,
            ).astype(jnp.bfloat16)
            key_part = jnp.einsum(
                "qk,qd->kd", grad_scores, query_rows, preferred_element_type=jnp.float32
            ).astype(jnp.bfloat16)
            return (query_part, row_delta, key_part, value_part)

        results = lax.map(head_back, (query_tile, key_block, value_block, grad_tile))
        query_part = results[0].transpose(1, 0, 2).reshape(TILE, channels)
        key_part = results[2].transpose(1, 0, 2).reshape(3, 3, TILE, channels)
        value_part = results[3].transpose(1, 0, 2).reshape(3, 3, TILE, channels)
        return (query_part, results[1], key_part, value_part)

    def guarded_own():
        blank_parts = (
            jnp.zeros((TILE, channels), jnp.bfloat16),
            jnp.zeros((heads_here, TILE), jnp.float32),
        )
        blank_parts = blank_parts + (
            jnp.zeros((3, 3, TILE, channels), jnp.bfloat16),
            jnp.zeros((3, 3, TILE, channels), jnp.bfloat16),
        )
        return own_side()

    def place_tile(carried, tile_index):
        query_part, row_delta, key_part, value_part = guarded_own()
        return ((key_part, value_part), query_part)

    empty_slots = jnp.zeros((3, 3, row_count, channels), jnp.bfloat16)
    (slots_key, slots_value), query_parts = lax.scan(
        place_tile, (empty_slots, empty_slots), tile_ids
    )
    middle_key = slots_key[1].astype(jnp.float32)
    middle_value = slots_value[1].astype(jnp.float32)
    for by_step, source in ((-1, 0), (1, 2)):
        moved_key, moved_value = from_behind(
            (slots_key[source], slots_value[source]), "ta", by_step
        )
        middle_key = middle_key + moved_key.astype(jnp.float32)
        middle_value = middle_value + moved_value.astype(jnp.float32)
    final_key = middle_key[1]
    final_value = middle_value[1]
    for by_step, source in ((-1, 0), (1, 2)):
        moved_key, moved_value = (
            from_behind(middle_key[source].astype(jnp.bfloat16), "ha", by_step).astype(jnp.float32),
            from_behind(middle_value[source].astype(jnp.bfloat16), "ha", by_step).astype(
                jnp.float32
            ),
        )
        final_key = final_key + moved_key
        final_value = final_value + moved_value
    key_grad = final_key.astype(jnp.bfloat16).reshape(1, 1, row_count, channels)
    value_grad = final_value.astype(jnp.bfloat16).reshape(1, 1, row_count, channels)
    query_grad = query_parts.reshape(1, 1, row_count, channels)
    return (
        stream_grad.reshape(1, 1, row_count, model_width),
        query_grad,
        key_grad,
        value_grad,
        out_weight_grad,
    )


def solution(mesh):
    placed = (
        P("ta", "ha", None, None),
        P("ta", "ha", None, "wa"),
        P("ta", "ha", None, "wa"),
        P("ta", "ha", None, "wa"),
        P("wa", None),
        P(),
        P(("ta", "ha"), "wa"),
        P("wa", ("ta", "ha")),
        P("ta", "ha", None),
        P("ta", "ha", None, None),
    )
    return jax.shard_map(
        shards,
        mesh=mesh,
        in_specs=placed,
        out_specs=(
            P("ta", "ha", None, None),
            P("ta", "ha", None, "wa"),
            P("ta", "ha", None, "wa"),
            P("ta", "ha", None, "wa"),
            P("wa", ("ta", "ha")),
        ),
        check_vma=False,
    )
```

profile of v0, /device:TPU:0, one launch (start us, length us, event | category | flops | bytes accessed | tf_op | source)
XLA Modules:
  0.0 548.8 jit_solution(6073854629250690570)
XLA Ops:
  30.7 6.4 %collective-permute-start.6 = (bf16[3,1,384,384]{3,2,1,0:T(8,128)(2,1)S(1)}, bf16[3,1,384,384]{3,2,1,0:T(8,128)(2,1)}, u32[]{:S(2)}, u32[]{:S(2)}) collective-permute-start(bf16[3,1,384,384]{3,2,1,0:T(8,128)(2,1)S(1)} %constant_dynamic-update-slice_fusion.1), channel_id=1, source_target_pairs={{0,4},{1,5},{2,6},{3,7},{8,12},{9,13},{10,14},{11,15},{16,20},{17,... | collective-permute-start | bytes 2654216 | tf_op jit(solution)/shard_map/ppermute | solution.py:23
  51.0 5.5 collective-permute-start.2
  56.6 6.5 %collective-permute-done.2 = bf16[3,1,1]{0,2,1:T(2,128)(2,1)S(1)} collective-permute-done((bf16[3,1,1]{0,2,1:T(2,128)(2,1)S(1)}, bf16[3,1,1]{0,2,1:T(2,128)(2,1)S(1)}, u32[]{:S(2)}, u32[]{:S(2)}) %collective-permute-start.2) | collective-permute-done | bytes 38 | tf_op jit(solution)/shard_map/ppermute | solution.py:23
  72.1 7.7 %reshape.147 = bf16[3456,3,128]{2,1,0:T(4,128)(2,1)} reshape(bf16[3,3,384,384]{3,2,1,0:T(8,128)(2,1)} %pad_maximum_fusion.1) | data formatting | bytes 5308416 | tf_op jit(solution)/shard_map/while/body/eval_jaxpr/reshape | solution.py:103
  87.0 7.7 %reshape.146 = bf16[3456,3,128]{2,1,0:T(4,128)(2,1)} reshape(bf16[3,3,384,384]{3,2,1,0:T(8,128)(2,1)} %pad_maximum_fusion) | data formatting | bytes 5308416 | tf_op jit(solution)/shard_map/while/body/eval_jaxpr/reshape | solution.py:102
  98.7 16.9 %while.44 = (s32[]{:T(128)}, f32[3,384,128]{1,2,0:T(8,128)S(1)}, bf16[3,384,128]{2,1,0:T(8,128)(2,1)S(1)}, bf16[3,3456,128]{2,1,0:T(8,128)(2,1)}, bf16[3,3456,128]{2,1,0:T(8,128)(2,1)}, /*index=5*/f32[9]{0:T(128)S(1)}, s32[]{:T(128)}) while((s32[]{:T(128)}, f32[3,384,128]{1,2,0:T(8,128)S(1)}, bf16[3,384,128]{2,1,0:T(8,128)(2,1)S(1)}, ...), condition=%wide.region_3.4_spmd.clone, body=%wide.region_0.3_spmd.clone.sunk | while | flops 690093312 | bytes 18014980 | solution.py:126
  118.0 32.4 %reduce-scatter.4.cloned.1.call-done = f32[96,1536]{1,0:T(8,128)} async-done(((f32[384,1536]{1,0:T(8,128)}), f32[96,1536]{1,0:T(8,128)}) %reduce-scatter.4.cloned.1.call-update) | async-done | bytes 589840 | tf_op jit(solution)/shard_map/reduce_scatter | solution.py:133
  154.7 15.8 %all-gather.7.cloned.1.call-done = bf16[384,1536]{1,0:T(8,128)(2,1)} async-done(((bf16[96,1536]{1,0:T(8,128)(2,1)}), bf16[384,1536]{1,0:T(8,128)(2,1)}) %all-gather.7.cloned.1.call-update) | async-done | bytes 1179664 | tf_op jit(solution)/shard_map/all_gather | solution.py:144
  170.5 82.3 %all-gather.9.cloned.1.call-done = bf16[1536,1536]{1,0:T(8,128)(2,1)} async-done(((bf16[192,1536]{1,0:T(8,128)(2,1)}), bf16[1536,1536]{1,0:T(8,128)(2,1)}) %all-gather.9.cloned.1.call-update) | async-done | bytes 4718608 | tf_op jit(solution)/shard_map/all_gather | solution.py:146
  252.8 6.1 %fusion.80 = f32[384,1536]{1,0:T(8,128)} fusion(bf16[384,1536]{1,0:T(8,128)(2,1)} %all-gather.7.cloned.1.call-done, bf16[1536,1536]{1,0:T(8,128)(2,1)} %all-gather.9.cloned.1.call-done), kind=kOutput, calls=%fused_computation.124 | convolution fusion | flops 1811939328 | bytes 8257536 | tf_op jit(solution)/shard_map/dot_general | solution.py:149
  258.9 74.3 %all-gather.5.cloned.1.call-done = bf16[1536,1536]{0,1:T(8,128)(2,1)} async-done(((bf16[1536,192]{0,1:T(8,128)(2,1)}), bf16[1536,1536]{0,1:T(8,128)(2,1)}) %all-gather.5.cloned.1.call-update) | async-done | bytes 4718608 | tf_op jit(solution)/shard_map/all_gather | solution.py:147
  333.1 10.0 %fusion.56 = f32[384,1536]{1,0:T(8,128)} fusion(bf16[1536,1536]{1,0:T(8,128)(2,1)} %all-gather.9.cloned.1.call-done, bf16[1536,1536]{0,1:T(8,128)(2,1)} %all-gather.5.cloned.1.call-done, f32[384,1536]{1,0:T(8,128)} %fusion.80, bf16[1,1,384,1536]{3,2,1,0:T(8,128)(2,1)} %param.23), kind=kOutput, calls=%fused_computation.75 | convolution fusion | flops 3635085312 | bytes 15335424 | tf_op jit(solution)/shard_map/tf,df->td/dot_general | solution.py:152
  343.3 31.3 %reduce-scatter.6.cloned.1.call-done = f32[96,1536]{1,0:T(8,128)} async-done(((f32[384,1536]{1,0:T(8,128)}), f32[96,1536]{1,0:T(8,128)}) %reduce-scatter.6.cloned.1.call-update) | async-done | bytes 589840 | tf_op jit(solution)/shard_map/reduce_scatter | solution.py:153
  378.2 17.5 %all-gather.11.cloned.1.call-done = bf16[384,1536]{1,0:T(8,128)(2,1)} async-done(((bf16[96,1536]{1,0:T(8,128)(2,1)}), bf16[384,1536]{1,0:T(8,128)(2,1)}) %all-gather.11.cloned.1.call-update) | async-done | bytes 1179664 | tf_op jit(solution)/shard_map/all_gather | solution.py:158
  400.5 43.7 %while.45 = (s32[]{:T(128)}, bf16[3,384,128]{1,2,0:T(8,128)(2,1)S(1)}, bf16[3,3456,128]{2,1,0:T(8,128)(2,1)}, bf16[3,3456,128]{2,1,0:T(8,128)(2,1)}, bf16[3,384,...) while((s32[]{:T(128)}, ...), condition=%wide.region_14.15_spmd.clone, body=%wide.region_10.14_spmd.clone.sunk | while | flops 1723513728 | bytes 71701848 | solution.py:197
  447.1 5.5 copy.58
  456.0 5.6 %copy.59 = bf16[1152,3,128]{2,1,0:T(4,128)(2,1)S(1)} copy(bf16[1152,3,128]{2,0,1:T(8,128)(2,1)} %get-tuple-element.257) | data formatting | bytes 1769472 | tf_op jit(solution)/shard_map/slice | solution.py:226
  463.6 5.5 collective-permute-start.17
  472.5 5.5 copy.55
  481.3 5.6 %copy.56 = bf16[1152,3,128]{2,1,0:T(4,128)(2,1)S(1)} copy(bf16[1152,3,128]{2,0,1:T(8,128)(2,1)} %get-tuple-element.260) | data formatting | bytes 1769472 | tf_op jit(solution)/shard_map/slice | solution.py:226
  488.9 5.7 %collective-permute-start.13 = (bf16[3,384,384]{2,1,0:T(8,128)(2,1)}, bf16[3,384,384]{2,1,0:T(8,128)(2,1)}, u32[]{:S(2)}, u32[]{:S(2)}) collective-permute-start(bf16[3,384,384]{2,1,0:T(8,128)(2,1)} %squeeze.56), channel_id=1, source_target_pairs={{0,8},{8,16},{16,24},{1,9},{9,17},{17,25},{2,10},{10,18},{18,26},{... | collective-permute-start | bytes 2654216 | tf_op jit(solution)/shard_map/ppermute | solution.py:35
  494.6 5.9 %copy.57 = f32[1152,3,128]{2,1,0:T(4,128)} copy(f32[1152,3,128]{2,0,1:T(8,128)S(1)} %get-tuple-element.258) | data formatting | bytes 3538944 | tf_op jit(solution)/shard_map/convert_element_type | solution.py:223
  504.8 5.9 %copy.54 = f32[1152,3,128]{2,1,0:T(4,128)} copy(f32[1152,3,128]{2,0,1:T(8,128)S(1)} %copy-done.2) | data formatting | bytes 3538944 | tf_op jit(solution)/shard_map/convert_element_type | solution.py:222
  529.5 5.3 collective-permute-start.15
  (182 shorter events, 179.1 us)
Async XLA Ops:
  7.2 143.2 %reduce-scatter.4.cloned.1.call-start = ((), (), s32[]{:S(2)}) async-start(), calls=%async_computation.4 | async-start | bytes 2949120 | tf_op jit(solution)/shard_map/reduce_scatter | solution.py:133
  7.2 12.6 %collective-permute-start.8 = (bf16[1,1,384,384]{3,2,1,0:T(8,128)(2,1)}, bf16[1,1,384,384]{3,2,1,0:T(8,128)(2,1)S(1)}, u32[]{:S(2)}, u32[]{:S(2)}) collective-permute-start(bf16[1,1,384,384]{3,2,1,0:T(8,128)(2,1)} %param.17), channel_id=1, source_target_pairs={{0,8},{8,16},{16,24},{1,9},{9,17},{17,25},{2,10},{10,18},{18,26},{... | collective-permute-start | bytes 884744 | tf_op jit(solution)/shard_map/ppermute | solution.py:23
  12.3 11.5 %collective-permute-start.9 = (bf16[1,1,384,384]{3,2,1,0:T(8,128)(2,1)}, bf16[1,1,384,384]{3,2,1,0:T(8,128)(2,1)S(1)}, u32[]{:S(2)}, u32[]{:S(2)}) collective-permute-start(bf16[1,1,384,384]{3,2,1,0:T(8,128)(2,1)} %param.17), channel_id=1, source_target_pairs={{8,0},{16,8},{24,16},{9,1},{17,9},{25,17},{10,2},{18,10},{26,18},{... | collective-permute-start | bytes 884744 | tf_op jit(solution)/shard_map/ppermute | solution.py:25
  13.6 15.9 %collective-permute-start.4 = (bf16[1,1,384,384]{3,2,1,0:T(8,128)(2,1)}, bf16[1,1,384,384]{3,2,1,0:T(8,128)(2,1)S(1)}, u32[]{:S(2)}, u32[]{:S(2)}) collective-permute-start(bf16[1,1,384,384]{3,2,1,0:T(8,128)(2,1)} %param.16), channel_id=1, source_target_pairs={{0,8},{8,16},{16,24},{1,9},{9,17},{17,25},{2,10},{10,18},{18,26},{... | collective-permute-start | bytes 884744 | tf_op jit(solution)/shard_map/ppermute | solution.py:23
  18.2 12.4 %collective-permute-start.5 = (bf16[1,1,384,384]{3,2,1,0:T(8,128)(2,1)}, bf16[1,1,384,384]{3,2,1,0:T(8,128)(2,1)S(1)}, u32[]{:S(2)}, u32[]{:S(2)}) collective-permute-start(bf16[1,1,384,384]{3,2,1,0:T(8,128)(2,1)} %param.16), channel_id=1, source_target_pairs={{8,0},{16,8},{24,16},{9,1},{17,9},{25,17},{10,2},{18,10},{26,18},{... | collective-permute-start | bytes 884744 | tf_op jit(solution)/shard_map/ppermute | solution.py:25
  23.9 44.9 %collective-permute-start.10 = (bf16[3,1,384,384]{3,2,1,0:T(8,128)(2,1)S(1)}, bf16[3,1,384,384]{3,2,1,0:T(8,128)(2,1)}, u32[]{:S(2)}, u32[]{:S(2)}) collective-permute-start(bf16[3,1,384,384]{3,2,1,0:T(8,128)(2,1)S(1)} %constant_dynamic-update-slice_fusion.4), channel_id=1, source_target_pairs={{0,4},{1,5},{2,6},{3,7},{8,12},{9,13},{10,14},{11,15},{16,20},{17,... | collective-permute-start | bytes 2654216 | tf_op jit(solution)/shard_map/ppermute | solution.py:23
  28.3 40.5 %collective-permute-start.11 = (bf16[3,1,384,384]{3,2,1,0:T(8,128)(2,1)S(1)}, bf16[3,1,384,384]{3,2,1,0:T(8,128)(2,1)}, u32[]{:S(2)}, u32[]{:S(2)}) collective-permute-start(bf16[3,1,384,384]{3,2,1,0:T(8,128)(2,1)S(1)} %constant_dynamic-update-slice_fusion.4), channel_id=1, source_target_pairs={{4,0},{5,1},{6,2},{7,3},{12,8},{13,9},{14,10},{15,11},{20,16},{21,... | collective-permute-start | bytes 2654216 | tf_op jit(solution)/shard_map/ppermute | solution.py:25
  30.7 53.0 %collective-permute-start.6 = (bf16[3,1,384,384]{3,2,1,0:T(8,128)(2,1)S(1)}, bf16[3,1,384,384]{3,2,1,0:T(8,128)(2,1)}, u32[]{:S(2)}, u32[]{:S(2)}) collective-permute-start(bf16[3,1,384,384]{3,2,1,0:T(8,128)(2,1)S(1)} %constant_dynamic-update-slice_fusion.1), channel_id=1, source_target_pairs={{0,4},{1,5},{2,6},{3,7},{8,12},{9,13},{10,14},{11,15},{16,20},{17,... | collective-permute-start | bytes 2654216 | tf_op jit(solution)/shard_map/ppermute | solution.py:23
  37.1 46.6 %collective-permute-start.7 = (bf16[3,1,384,384]{3,2,1,0:T(8,128)(2,1)S(1)}, bf16[3,1,384,384]{3,2,1,0:T(8,128)(2,1)}, u32[]{:S(2)}, u32[]{:S(2)}) collective-permute-start(bf16[3,1,384,384]{3,2,1,0:T(8,128)(2,1)S(1)} %constant_dynamic-update-slice_fusion.1), channel_id=1, source_target_pairs={{4,0},{5,1},{6,2},{7,3},{12,8},{13,9},{14,10},{15,11},{20,16},{21,... | collective-permute-start | bytes 2654216 | tf_op jit(solution)/shard_map/ppermute | solution.py:25
  51.0 12.1 %collective-permute-start.2 = (bf16[3,1,1]{0,2,1:T(2,128)(2,1)S(1)}, bf16[3,1,1]{0,2,1:T(2,128)(2,1)S(1)}, u32[]{:S(2)}, u32[]{:S(2)}) collective-permute-start(bf16[3,1,1]{0,2,1:T(2,128)(2,1)S(1)} %pad_maximum_fusion.2), channel_id=1, source_target_pairs={{0,4},{1,5},{2,6},{3,7},{8,12},{9,13},{10,14},{11,15},{16,20},{17,... | collective-permute-start | bytes 26 | tf_op jit(solution)/shard_map/ppermute | solution.py:23
  117.9 52.5 %all-gather.7.cloned.1.call-start = ((), (), s32[]{:S(2)}) async-start(), calls=%async_computation.5 | async-start | bytes 1474560 | tf_op jit(solution)/shard_map/all_gather | solution.py:144
  152.8 100.0 %all-gather.9.cloned.1.call-start = ((), (), s32[]{:S(2)}) async-start(), calls=%async_computation.6 | async-start | bytes 5308416 | tf_op jit(solution)/shard_map/all_gather | solution.py:146
  153.6 179.6 %all-gather.5.cloned.1.call-start = ((), (), s32[]{:S(2)}) async-start(), calls=%async_computation.3 | async-start | bytes 5308416 | tf_op jit(solution)/shard_map/all_gather | solution.py:147
  154.2 220.4 %reduce-scatter.6.cloned.1.call-start = ((), (), s32[]{:S(2)}) async-start(), calls=%async_computation.7 | async-start | bytes 2949120 | tf_op jit(solution)/shard_map/reduce_scatter | solution.py:153
  343.2 52.6 %all-gather.11.cloned.1.call-start = ((), (), s32[]{:S(2)}) async-start(), calls=%async_computation.8 | async-start | bytes 1474560 | tf_op jit(solution)/shard_map/all_gather | solution.py:158
  378.1 162.6 %reduce-scatter.8.cloned.1.call-start = ((), (), s32[]{:S(2)}) async-start(), calls=%async_computation.9 | async-start | bytes 2654208 | tf_op jit(solution)/shard_map/reduce_scatter | solution.py:162
  454.6 59.0 %collective-permute-start.16 = (bf16[3,384,384]{2,1,0:T(8,128)(2,1)}, bf16[3,384,384]{2,1,0:T(8,128)(2,1)}, u32[]{:S(2)}, u32[]{:S(2)}) collective-permute-start(bf16[3,384,384]{2,1,0:T(8,128)(2,1)} %squeeze.58), channel_id=1, source_target_pairs={{8,0},{16,8},{24,16},{9,1},{17,9},{25,17},{10,2},{18,10},{26,18},{... | collective-permute-start | bytes 2654216 | tf_op jit(solution)/shard_map/ppermute | solution.py:35
  463.6 50.0 %collective-permute-start.17 = (bf16[3,384,384]{2,1,0:T(8,128)(2,1)}, bf16[3,384,384]{2,1,0:T(8,128)(2,1)}, u32[]{:S(2)}, u32[]{:S(2)}) collective-permute-start(bf16[3,384,384]{2,1,0:T(8,128)(2,1)} %squeeze.59), channel_id=1, source_target_pairs={{0,8},{8,16},{16,24},{1,9},{9,17},{17,25},{2,10},{10,18},{18,26},{... | collective-permute-start | bytes 2654216 | tf_op jit(solution)/shard_map/ppermute | solution.py:35
  480.0 44.5 %collective-permute-start.12 = (bf16[3,384,384]{2,1,0:T(8,128)(2,1)}, bf16[3,384,384]{2,1,0:T(8,128)(2,1)}, u32[]{:S(2)}, u32[]{:S(2)}) collective-permute-start(bf16[3,384,384]{2,1,0:T(8,128)(2,1)} %squeeze.55), channel_id=1, source_target_pairs={{8,0},{16,8},{24,16},{9,1},{17,9},{25,17},{10,2},{18,10},{26,18},{... | collective-permute-start | bytes 2654216 | tf_op jit(solution)/shard_map/ppermute | solution.py:35
  488.9 35.6 %collective-permute-start.13 = (bf16[3,384,384]{2,1,0:T(8,128)(2,1)}, bf16[3,384,384]{2,1,0:T(8,128)(2,1)}, u32[]{:S(2)}, u32[]{:S(2)}) collective-permute-start(bf16[3,384,384]{2,1,0:T(8,128)(2,1)} %squeeze.56), channel_id=1, source_target_pairs={{0,8},{8,16},{16,24},{1,9},{9,17},{17,25},{2,10},{10,18},{18,26},{... | collective-permute-start | bytes 2654216 | tf_op jit(solution)/shard_map/ppermute | solution.py:35
  517.9 17.8 %collective-permute-start.18 = (bf16[384,384]{1,0:T(8,128)(2,1)}, bf16[384,384]{1,0:T(8,128)(2,1)S(1)}, u32[]{:S(2)}, u32[]{:S(2)}) collective-permute-start(bf16[384,384]{1,0:T(8,128)(2,1)} %get-tuple-element.262), channel_id=1, source_target_pairs={{4,0},{5,1},{6,2},{7,3},{12,8},{13,9},{14,10},{15,11},{20,16},{21,... | collective-permute-start | bytes 884744 | tf_op jit(solution)/shard_map/ppermute | solution.py:35
  519.2 16.5 %collective-permute-start.19 = (bf16[384,384]{1,0:T(8,128)(2,1)S(1)}, bf16[384,384]{1,0:T(8,128)(2,1)}, u32[]{:S(2)}, u32[]{:S(2)}) collective-permute-start(bf16[384,384]{1,0:T(8,128)(2,1)S(1)} %get-tuple-element.263), channel_id=1, source_target_pairs={{0,4},{1,5},{2,6},{3,7},{8,12},{9,13},{10,14},{11,15},{16,20},{17,... | collective-permute-start | bytes 884744 | tf_op jit(solution)/shard_map/ppermute | solution.py:35
  528.2 9.5 %collective-permute-start.14 = (bf16[384,384]{1,0:T(8,128)(2,1)}, bf16[384,384]{1,0:T(8,128)(2,1)S(1)}, u32[]{:S(2)}, u32[]{:S(2)}) collective-permute-start(bf16[384,384]{1,0:T(8,128)(2,1)} %get-tuple-element.264), channel_id=1, source_target_pairs={{4,0},{5,1},{6,2},{7,3},{12,8},{13,9},{14,10},{15,11},{20,16},{21,... | collective-permute-start | bytes 884744 | tf_op jit(solution)/shard_map/ppermute | solution.py:35
  529.5 9.2 %collective-permute-start.15 = (bf16[384,384]{1,0:T(8,128)(2,1)S(1)}, bf16[384,384]{1,0:T(8,128)(2,1)}, u32[]{:S(2)}, u32[]{:S(2)}) collective-permute-start(bf16[384,384]{1,0:T(8,128)(2,1)S(1)} %get-tuple-element.265), channel_id=1, source_target_pairs={{0,4},{1,5},{2,6},{3,7},{8,12},{9,13},{10,14},{11,15},{16,20},{17,... | collective-permute-start | bytes 884744 | tf_op jit(solution)/shard_map/ppermute | solution.py:35
  (17 other events, 235.4 us)
Sparse Core Ops, SparseCore 0:
  118.1 32.2 reduce-scatter.3
  153.0 17.4 all-gather.6
  172.9 79.8 all-gather.8
  255.1 78.0 all-gather.4
  343.3 31.1 reduce-scatter.5
  378.3 17.4 all-gather.10
  400.6 72.8 reduce-scatter.7
where the time goes:
time: 557 us; the launch traced here: 549 us
  waiting for transfers between devices  274 us (49%)
  local copies, waits for them, and re-layouts  84.7 us (15%)
  matrix products  66.8 us (12%)
  starting transfers between devices  66.1 us (12%)
  other arithmetic  41.6 us (7%)
  between operations  15.4 us (3%)
    all_gather x1, waiting for transfers between devices, shards(): lax.all_gather(up_weight, ('ta', 'ha'), axis=0, tiled=True)  82.3 us
    all_gather x1, waiting for transfers between devices, shards(): lax.all_gather(down_weight, ('ta', 'ha'), axis=1, tiled=True)  74.3 us
    reduce_scatter x1, waiting for transfers between devices, shards(): lax.psum_scatter(attn_part, 'wa', scatter_dimension=0, tiled=True)  32.4 us
    reduce_scatter x1, waiting for transfers between devices, shards(): lax.psum_scatter(norm_part, 'wa', scatter_dimension=0, tiled=True)  31.3 us
    ppermute x6, starting transfers between devices, extended(): lax.ppermute(tail, axis, [(i, (i + 1) % count) for i in range(ends)])  30.7 us
    ppermute x8, starting transfers between devices, from_behind(): return lax.ppermute(array, axis, pairs)  27 us
    all_gather x1, waiting for transfers between devices, shards(): stream_grad = lax.all_gather(grad_share, 'wa', axis=0, tiled=True)  17.5 us
    all_gather x1, waiting for transfers between devices, shards(): hidden_in = lax.all_gather(hidden_share, 'wa', axis=0, tiled=True)  15.8 us
  transfers between devices with their start and end apart: 27, of which 12 were waited for; matrix products, arithmetic and copies ran while one was open for 24% of the time, Pallas kernels for 0%

commit v1 on v0

--- a/solution.py
+++ b/solution.py
@@ -10,6 +10,28 @@
 TANH_SCALE = 0.7978845608028654
 CUBIC_COEF = 0.044715
 NEG_FILL = -1e30
+
+
+def laid_out(blocks, dim):
+    blocks = jnp.moveaxis(blocks, 0, dim)
+    shape = blocks.shape
+    return blocks.reshape(*shape[:dim], shape[dim] * shape[dim + 1], *shape[dim + 2 :])
+
+
+def gather_around(x, axis, dim):
+    count = lax.axis_size(axis)
+    pairs = [(i, (i + 1) % count) for i in range(count)]
+    back = [(b, a) for a, b in pairs]
+    lower, upper = ([], [])
+    for lap in range(count - 1):
+        if lap % 2 == 0:
+            lower.append(lax.ppermute(lower[-1] if lower else x, axis, pairs))
+        else:
+            upper.append(lax.ppermute(upper[-1] if upper else x, axis, back))
+    blocks = jnp.stack([*lower[::-1], x, *upper])
+    shift = lax.axis_index(axis) - len(lower)
+    blocks = blocks[(jnp.arange(count) - shift) % count]
+    return laid_out(blocks, dim)
 
 
 def extended(cells, sides, width):
@@ -141,7 +163,7 @@
     )
     normed, inv_std = layer_norm(residual)
     hidden_share = (normed * norm_gain).astype(jnp.bfloat16)
-    hidden_in = lax.all_gather(hidden_share, "wa", axis=0, tiled=True)
+    hidden_in = gather_around(hidden_share, "wa", 0)
     up_full, down_full = (
         lax.all_gather(up_weight, ("ta", "ha"), axis=0, tiled=True),
         lax.all_gather(down_weight, ("ta", "ha"), axis=1, tiled=True),

time: 557 us -> 508 us (0.912)
  waiting for transfers between devices: 274 us -> 216 us
    all_gather x1, waiting for transfers between devices: 82.3 us -> 29.9 us  [shards(): lax.all_gather(up_weight, ('ta', 'ha'), axis=0, tiled=True)]
    all_gather x1 -> x0, waiting for transfers between devices: 15.8 us -> none  [shards(): hidden_in = lax.all_gather(hidden_share, 'wa', axis=0, tiled=True)]
    ppermute x0 -> x3, waiting for transfers between devices: none -> 11.7 us  [the longest x2 11.7 us: gather_around(): lower.append(lax.ppermute(lower[-1] if lower else x, axis, pairs))]
    unnamed x26 -> x38, local copies, waits for them, and re-layouts: 12.3 us -> 13.5 us
  transfers between devices with their start and end apart: 27 -> 29, of which waited for: 12 -> 14; matrix products, arithmetic and copies ran while one was open for 24% -> 28% of each run, Pallas kernels for 0% -> 0%
where the time goes in v1:
time: 508 us; the launch traced here: 499 us
  waiting for transfers between devices  216 us (43%)
  local copies, waits for them, and re-layouts  88.5 us (17%)
  starting transfers between devices  68 us (13%)
  matrix products  67.1 us (13%)
  other arithmetic  42.7 us (8%)
  between operations  16.8 us (3%)
    all_gather x1, waiting for transfers between devices, shards(): lax.all_gather(down_weight, ('ta', 'ha'), axis=1, tiled=True)  73.9 us
    reduce_scatter x1, waiting for transfers between devices, shards(): lax.psum_scatter(norm_part, 'wa', scatter_dimension=0, tiled=True)  31.4 us
    reduce_scatter x1, waiting for transfers between devices, shards(): lax.psum_scatter(attn_part, 'wa', scatter_dimension=0, tiled=True)  31.3 us
    ppermute x6, starting transfers between devices, extended(): lax.ppermute(tail, axis, [(i, (i + 1) % count) for i in range(ends)])  30.7 us
    all_gather x1, waiting for transfers between devices, shards(): lax.all_gather(up_weight, ('ta', 'ha'), axis=0, tiled=True)  29.9 us
    ppermute x8, starting transfers between devices, from_behind(): return lax.ppermute(array, axis, pairs)  27.2 us
    all_gather x1, waiting for transfers between devices, shards(): stream_grad = lax.all_gather(grad_share, 'wa', axis=0, tiled=True)  17.6 us
    unnamed x38, local copies, waits for them, and re-layouts  13.5 us
  transfers between devices with their start and end apart: 29, of which 14 were waited for; matrix products, arithmetic and copies ran while one was open for 28% of the time, Pallas kernels for 0%

profile of v1, /device:TPU:0, one launch (start us, length us, event | category | flops | bytes accessed | tf_op | source)
XLA Modules:
  0.0 499.4 jit_solution(17781928242858018217)
XLA Ops:
  31.5 6.4 %collective-permute-start.6 = (bf16[3,1,384,384]{3,2,1,0:T(8,128)(2,1)S(1)}, bf16[3,1,384,384]{3,2,1,0:T(8,128)(2,1)}, u32[]{:S(2)}, u32[]{:S(2)}) collective-permute-start(bf16[3,1,384,384]{3,2,1,0:T(8,128)(2,1)S(1)} %constant_dynamic-update-slice_fusion.1), channel_id=1, source_target_pairs={{0,4},{1,5},{2,6},{3,7},{8,12},{9,13},{10,14},{11,15},{16,20},{17,... | collective-permute-start | bytes 2654216 | tf_op jit(solution)/shard_map/ppermute | solution.py:45
  51.9 5.5 %collective-permute-start.2 = (bf16[3,1,1]{0,2,1:T(2,128)(2,1)S(1)}, bf16[3,1,1]{0,2,1:T(2,128)(2,1)S(1)}, u32[]{:S(2)}, u32[]{:S(2)}) collective-permute-start(bf16[3,1,1]{0,2,1:T(2,128)(2,1)S(1)} %pad_maximum_fusion.3), channel_id=1, source_target_pairs={{0,4},{1,5},{2,6},{3,7},{8,12},{9,13},{10,14},{11,15},{16,20},{17,... | collective-permute-start | bytes 26 | tf_op jit(solution)/shard_map/ppermute | solution.py:45
  57.4 6.5 %collective-permute-done.2 = bf16[3,1,1]{0,2,1:T(2,128)(2,1)S(1)} collective-permute-done((bf16[3,1,1]{0,2,1:T(2,128)(2,1)S(1)}, bf16[3,1,1]{0,2,1:T(2,128)(2,1)S(1)}, u32[]{:S(2)}, u32[]{:S(2)}) %collective-permute-start.2) | collective-permute-done | bytes 38 | tf_op jit(solution)/shard_map/ppermute | solution.py:45
  72.9 7.7 %reshape.199 = bf16[3456,3,128]{2,1,0:T(4,128)(2,1)} reshape(bf16[3,3,384,384]{3,2,1,0:T(8,128)(2,1)} %pad_maximum_fusion.1) | data formatting | bytes 5308416 | tf_op jit(solution)/shard_map/while/body/eval_jaxpr/reshape | solution.py:125
  87.9 7.7 %reshape.198 = bf16[3456,3,128]{2,1,0:T(4,128)(2,1)} reshape(bf16[3,3,384,384]{3,2,1,0:T(8,128)(2,1)} %pad_maximum_fusion) | data formatting | bytes 5308416 | tf_op jit(solution)/shard_map/while/body/eval_jaxpr/reshape | solution.py:124
  99.6 16.9 %while.44 = (s32[]{:T(128)}, f32[3,384,128]{1,2,0:T(8,128)S(1)}, bf16[3,384,128]{2,1,0:T(8,128)(2,1)S(1)}, bf16[3,3456,128]{2,1,0:T(8,128)(2,1)}, bf16[3,3456,128]{2,1,0:T(8,128)(2,1)}, /*index=5*/f32[9]{0:T(128)S(1)}, s32[]{:T(128)}) while((s32[]{:T(128)}, f32[3,384,128]{1,2,0:T(8,128)S(1)}, bf16[3,384,128]{2,1,0:T(8,128)(2,1)S(1)}, ...), condition=%wide.region_3.4_spmd.clone, body=%wide.region_0.3_spmd.clone.sunk | while | flops 690093312 | bytes 18014980 | solution.py:148
  120.5 31.3 %reduce-scatter.4.cloned.1.call-done = f32[96,1536]{1,0:T(8,128)} async-done(((f32[384,1536]{1,0:T(8,128)}), f32[96,1536]{1,0:T(8,128)}) %reduce-scatter.4.cloned.1.call-update) | async-done | bytes 589840 | tf_op jit(solution)/shard_map/reduce_scatter | solution.py:155
  156.0 5.7 %collective-permute-done.12 = bf16[96,1536]{1,0:T(8,128)(2,1)S(1)} collective-permute-done((bf16[96,1536]{1,0:T(8,128)(2,1)S(1)}, bf16[96,1536]{1,0:T(8,128)(2,1)S(1)}, u32[]{:S(2)}, u32[]{:S(2)}) %collective-permute-start.12) | collective-permute-done | bytes 294944 | tf_op jit(solution)/shard_map/ppermute | solution.py:28
  162.3 6.0 %collective-permute-done.13 = bf16[96,1536]{1,0:T(8,128)(2,1)S(1)} collective-permute-done((bf16[96,1536]{1,0:T(8,128)(2,1)S(1)}, bf16[96,1536]{1,0:T(8,128)(2,1)S(1)}, u32[]{:S(2)}, u32[]{:S(2)}) %collective-permute-start.13) | collective-permute-done | bytes 294944 | tf_op jit(solution)/shard_map/ppermute | solution.py:28
  171.1 29.9 %all-gather.6.cloned.1.call-done = bf16[1536,1536]{1,0:T(8,128)(2,1)} async-done(((bf16[192,1536]{1,0:T(8,128)(2,1)}), bf16[1536,1536]{1,0:T(8,128)(2,1)}) %all-gather.6.cloned.1.call-update) | async-done | bytes 4718608 | tf_op jit(solution)/shard_map/all_gather | solution.py:168
  201.0 6.2 %fusion.82 = f32[384,1536]{1,0:T(8,128)} fusion(bf16[384,1536]{1,0:T(8,128)(2,1)} %bitcast.182, bf16[1536,1536]{1,0:T(8,128)(2,1)} %all-gather.6.cloned.1.call-done), kind=kOutput, calls=%fused_computation.133 | convolution fusion | flops 1811939328 | bytes 8257536 | tf_op jit(solution)/shard_map/dot_general | solution.py:171
  207.2 73.9 %all-gather.4.cloned.1.call-done = bf16[1536,1536]{0,1:T(8,128)(2,1)} async-done(((bf16[1536,192]{0,1:T(8,128)(2,1)}), bf16[1536,1536]{0,1:T(8,128)(2,1)}) %all-gather.4.cloned.1.call-update) | async-done | bytes 4718608 | tf_op jit(solution)/shard_map/all_gather | solution.py:169
  281.0 9.6 %fusion.56 = f32[384,1536]{1,0:T(8,128)} fusion(bf16[1536,1536]{1,0:T(8,128)(2,1)} %all-gather.6.cloned.1.call-done, bf16[1536,1536]{0,1:T(8,128)(2,1)} %all-gather.4.cloned.1.call-done, f32[384,1536]{1,0:T(8,128)} %fusion.82, bf16[1,1,384,1536]{3,2,1,0:T(8,128)(2,1)S(1)} %copy-done.13), kind=kOutput, calls=%fused_computation.77 | convolution fusion | flops 3635085312 | bytes 15335424 | tf_op jit(solution)/shard_map/tf,df->td/dot_general | solution.py:174
  290.7 31.4 %reduce-scatter.6.cloned.1.call-done = f32[96,1536]{1,0:T(8,128)} async-done(((f32[384,1536]{1,0:T(8,128)}), f32[96,1536]{1,0:T(8,128)}) %reduce-scatter.6.cloned.1.call-update) | async-done | bytes 589840 | tf_op jit(solution)/shard_map/reduce_scatter | solution.py:175
  325.7 17.6 %all-gather.8.cloned.1.call-done = bf16[384,1536]{1,0:T(8,128)(2,1)} async-done(((bf16[96,1536]{1,0:T(8,128)(2,1)}), bf16[384,1536]{1,0:T(8,128)(2,1)}) %all-gather.8.cloned.1.call-update) | async-done | bytes 1179664 | tf_op jit(solution)/shard_map/all_gather | solution.py:180
  349.7 43.6 %while.45 = (s32[]{:T(128)}, bf16[3,384,128]{1,2,0:T(8,128)(2,1)S(1)}, bf16[3,3456,128]{2,1,0:T(8,128)(2,1)}, bf16[3,3456,128]{2,1,0:T(8,128)(2,1)}, bf16[3,384,...) while((s32[]{:T(128)}, ...), condition=%wide.region_14.15_spmd.clone, body=%wide.region_10.14_spmd.clone.sunk | while | flops 1723513728 | bytes 71701848 | solution.py:219
  396.9 5.5 %copy.58 = bf16[1152,3,128]{2,1,0:T(4,128)(2,1)S(1)} copy(bf16[1152,3,128]{2,0,1:T(8,128)(2,1)S(1)} %get-tuple-element.256) | data formatting | bytes 1769472 | tf_op jit(solution)/shard_map/slice | solution.py:248
  405.8 5.6 %copy.59 = bf16[1152,3,128]{2,1,0:T(4,128)(2,1)S(1)} copy(bf16[1152,3,128]{2,0,1:T(8,128)(2,1)} %get-tuple-element.257) | data formatting | bytes 1769472 | tf_op jit(solution)/shard_map/slice | solution.py:248
  413.4 5.5 %collective-permute-start.20 = (bf16[3,384,384]{2,1,0:T(8,128)(2,1)}, bf16[3,384,384]{2,1,0:T(8,128)(2,1)}, u32[]{:S(2)}, u32[]{:S(2)}) collective-permute-start(bf16[3,384,384]{2,1,0:T(8,128)(2,1)} %squeeze.59), channel_id=1, source_target_pairs={{0,8},{8,16},{16,24},{1,9},{9,17},{17,25},{2,10},{10,18},{18,26},{... | collective-permute-start | bytes 2654216 | tf_op jit(solution)/shard_map/ppermute | solution.py:57
  422.4 5.5 %copy.55 = bf16[1152,3,128]{2,1,0:T(4,128)(2,1)S(1)} copy(bf16[1152,3,128]{2,0,1:T(8,128)(2,1)S(1)} %get-tuple-element.259) | data formatting | bytes 1769472 | tf_op jit(solution)/shard_map/slice | solution.py:248
  431.1 5.6 %copy.56 = bf16[1152,3,128]{2,1,0:T(4,128)(2,1)S(1)} copy(bf16[1152,3,128]{2,0,1:T(8,128)(2,1)} %get-tuple-element.260) | data formatting | bytes 1769472 | tf_op jit(solution)/shard_map/slice | solution.py:248
  438.7 5.7 %collective-permute-start.16 = (bf16[3,384,384]{2,1,0:T(8,128)(2,1)}, bf16[3,384,384]{2,1,0:T(8,128)(2,1)}, u32[]{:S(2)}, u32[]{:S(2)}) collective-permute-start(bf16[3,384,384]{2,1,0:T(8,128)(2,1)} %squeeze.56), channel_id=1, source_target_pairs={{0,8},{8,16},{16,24},{1,9},{9,17},{17,25},{2,10},{10,18},{18,26},{... | collective-permute-start | bytes 2654216 | tf_op jit(solution)/shard_map/ppermute | solution.py:57
  444.3 5.9 %copy.57 = f32[1152,3,128]{2,1,0:T(4,128)} copy(f32[1152,3,128]{2,0,1:T(8,128)S(1)} %get-tuple-element.258) | data formatting | bytes 3538944 | tf_op jit(solution)/shard_map/convert_element_type | solution.py:245
  454.5 5.9 %copy.54 = f32[1152,3,128]{2,1,0:T(4,128)} copy(f32[1152,3,128]{2,0,1:T(8,128)S(1)} %copy-done.2) | data formatting | bytes 3538944 | tf_op jit(solution)/shard_map/convert_element_type | solution.py:244
  (202 shorter events, 191.8 us)
Async XLA Ops:
  8.0 143.8 %reduce-scatter.4.cloned.1.call-start = ((), (), s32[]{:S(2)}) async-start(), calls=%async_computation.4 | async-start | bytes 2949120 | tf_op jit(solution)/shard_map/reduce_scatter | solution.py:155
  8.1 12.6 %collective-permute-start.8 = (bf16[1,1,384,384]{3,2,1,0:T(8,128)(2,1)}, bf16[1,1,384,384]{3,2,1,0:T(8,128)(2,1)S(1)}, u32[]{:S(2)}, u32[]{:S(2)}) collective-permute-start(bf16[1,1,384,384]{3,2,1,0:T(8,128)(2,1)} %param.17), channel_id=1, source_target_pairs={{0,8},{8,16},{16,24},{1,9},{9,17},{17,25},{2,10},{10,18},{18,26},{... | collective-permute-start | bytes 884744 | tf_op jit(solution)/shard_map/ppermute | solution.py:45
  13.2 11.5 %collective-permute-start.9 = (bf16[1,1,384,384]{3,2,1,0:T(8,128)(2,1)}, bf16[1,1,384,384]{3,2,1,0:T(8,128)(2,1)S(1)}, u32[]{:S(2)}, u32[]{:S(2)}) collective-permute-start(bf16[1,1,384,384]{3,2,1,0:T(8,128)(2,1)} %param.17), channel_id=1, source_target_pairs={{8,0},{16,8},{24,16},{9,1},{17,9},{25,17},{10,2},{18,10},{26,18},{... | collective-permute-start | bytes 884744 | tf_op jit(solution)/shard_map/ppermute | solution.py:47
  14.5 15.9 %collective-permute-start.4 = (bf16[1,1,384,384]{3,2,1,0:T(8,128)(2,1)}, bf16[1,1,384,384]{3,2,1,0:T(8,128)(2,1)S(1)}, u32[]{:S(2)}, u32[]{:S(2)}) collective-permute-start(bf16[1,1,384,384]{3,2,1,0:T(8,128)(2,1)} %param.16), channel_id=1, source_target_pairs={{0,8},{8,16},{16,24},{1,9},{9,17},{17,25},{2,10},{10,18},{18,26},{... | collective-permute-start | bytes 884744 | tf_op jit(solution)/shard_map/ppermute | solution.py:45
  19.0 12.4 %collective-permute-start.5 = (bf16[1,1,384,384]{3,2,1,0:T(8,128)(2,1)}, bf16[1,1,384,384]{3,2,1,0:T(8,128)(2,1)S(1)}, u32[]{:S(2)}, u32[]{:S(2)}) collective-permute-start(bf16[1,1,384,384]{3,2,1,0:T(8,128)(2,1)} %param.16), channel_id=1, source_target_pairs={{8,0},{16,8},{24,16},{9,1},{17,9},{25,17},{10,2},{18,10},{26,18},{... | collective-permute-start | bytes 884744 | tf_op jit(solution)/shard_map/ppermute | solution.py:47
  24.7 44.9 %collective-permute-start.10 = (bf16[3,1,384,384]{3,2,1,0:T(8,128)(2,1)S(1)}, bf16[3,1,384,384]{3,2,1,0:T(8,128)(2,1)}, u32[]{:S(2)}, u32[]{:S(2)}) collective-permute-start(bf16[3,1,384,384]{3,2,1,0:T(8,128)(2,1)S(1)} %constant_dynamic-update-slice_fusion.4), channel_id=1, source_target_pairs={{0,4},{1,5},{2,6},{3,7},{8,12},{9,13},{10,14},{11,15},{16,20},{17,... | collective-permute-start | bytes 2654216 | tf_op jit(solution)/shard_map/ppermute | solution.py:45
  29.1 40.5 %collective-permute-start.11 = (bf16[3,1,384,384]{3,2,1,0:T(8,128)(2,1)S(1)}, bf16[3,1,384,384]{3,2,1,0:T(8,128)(2,1)}, u32[]{:S(2)}, u32[]{:S(2)}) collective-permute-start(bf16[3,1,384,384]{3,2,1,0:T(8,128)(2,1)S(1)} %constant_dynamic-update-slice_fusion.4), channel_id=1, source_target_pairs={{4,0},{5,1},{6,2},{7,3},{12,8},{13,9},{14,10},{15,11},{20,16},{21,... | collective-permute-start | bytes 2654216 | tf_op jit(solution)/shard_map/ppermute | solution.py:47
  31.5 53.1 %collective-permute-start.6 = (bf16[3,1,384,384]{3,2,1,0:T(8,128)(2,1)S(1)}, bf16[3,1,384,384]{3,2,1,0:T(8,128)(2,1)}, u32[]{:S(2)}, u32[]{:S(2)}) collective-permute-start(bf16[3,1,384,384]{3,2,1,0:T(8,128)(2,1)S(1)} %constant_dynamic-update-slice_fusion.1), channel_id=1, source_target_pairs={{0,4},{1,5},{2,6},{3,7},{8,12},{9,13},{10,14},{11,15},{16,20},{17,... | collective-permute-start | bytes 2654216 | tf_op jit(solution)/shard_map/ppermute | solution.py:45
  37.9 46.6 %collective-permute-start.7 = (bf16[3,1,384,384]{3,2,1,0:T(8,128)(2,1)S(1)}, bf16[3,1,384,384]{3,2,1,0:T(8,128)(2,1)}, u32[]{:S(2)}, u32[]{:S(2)}) collective-permute-start(bf16[3,1,384,384]{3,2,1,0:T(8,128)(2,1)S(1)} %constant_dynamic-update-slice_fusion.1), channel_id=1, source_target_pairs={{4,0},{5,1},{6,2},{7,3},{12,8},{13,9},{14,10},{15,11},{20,16},{21,... | collective-permute-start | bytes 2654216 | tf_op jit(solution)/shard_map/ppermute | solution.py:47
  51.9 12.1 %collective-permute-start.2 = (bf16[3,1,1]{0,2,1:T(2,128)(2,1)S(1)}, bf16[3,1,1]{0,2,1:T(2,128)(2,1)S(1)}, u32[]{:S(2)}, u32[]{:S(2)}) collective-permute-start(bf16[3,1,1]{0,2,1:T(2,128)(2,1)S(1)} %pad_maximum_fusion.3), channel_id=1, source_target_pairs={{0,4},{1,5},{2,6},{3,7},{8,12},{9,13},{10,14},{11,15},{16,20},{17,... | collective-permute-start | bytes 26 | tf_op jit(solution)/shard_map/ppermute | solution.py:45
  119.3 81.7 %all-gather.6.cloned.1.call-start = ((), (), s32[]{:S(2)}) async-start(), calls=%async_computation.5 | async-start | bytes 5308416 | tf_op jit(solution)/shard_map/all_gather | solution.py:168
  119.9 161.1 %all-gather.4.cloned.1.call-start = ((), (), s32[]{:S(2)}) async-start(), calls=%async_computation.3 | async-start | bytes 5308416 | tf_op jit(solution)/shard_map/all_gather | solution.py:169
  120.5 201.6 %reduce-scatter.6.cloned.1.call-start = ((), (), s32[]{:S(2)}) async-start(), calls=%async_computation.6 | async-start | bytes 2949120 | tf_op jit(solution)/shard_map/reduce_scatter | solution.py:175
  153.5 8.1 %collective-permute-start.12 = (bf16[96,1536]{1,0:T(8,128)(2,1)S(1)}, bf16[96,1536]{1,0:T(8,128)(2,1)S(1)}, u32[]{:S(2)}, u32[]{:S(2)}) collective-permute-start(bf16[96,1536]{1,0:T(8,128)(2,1)S(1)} %multiply_convert_fusion.1), channel_id=1, source_target_pairs={{0,1},{1,2},{2,3},{3,0},{4,5},{5,6},{6,7},{7,4},{8,9},{9,10},{10,1... | collective-permute-start | bytes 884744 | tf_op jit(solution)/shard_map/ppermute | solution.py:28
  290.7 52.6 %all-gather.8.cloned.1.call-start = ((), (), s32[]{:S(2)}) async-start(), calls=%async_computation.7 | async-start | bytes 1474560 | tf_op jit(solution)/shard_map/all_gather | solution.py:180
  325.6 165.2 %reduce-scatter.8.cloned.1.call-start = ((), (), s32[]{:S(2)}) async-start(), calls=%async_computation.8 | async-start | bytes 2654208 | tf_op jit(solution)/shard_map/reduce_scatter | solution.py:184
  404.4 59.0 %collective-permute-start.19 = (bf16[3,384,384]{2,1,0:T(8,128)(2,1)}, bf16[3,384,384]{2,1,0:T(8,128)(2,1)}, u32[]{:S(2)}, u32[]{:S(2)}) collective-permute-start(bf16[3,384,384]{2,1,0:T(8,128)(2,1)} %squeeze.58), channel_id=1, source_target_pairs={{8,0},{16,8},{24,16},{9,1},{17,9},{25,17},{10,2},{18,10},{26,18},{... | collective-permute-start | bytes 2654216 | tf_op jit(solution)/shard_map/ppermute | solution.py:57
  413.4 50.0 %collective-permute-start.20 = (bf16[3,384,384]{2,1,0:T(8,128)(2,1)}, bf16[3,384,384]{2,1,0:T(8,128)(2,1)}, u32[]{:S(2)}, u32[]{:S(2)}) collective-permute-start(bf16[3,384,384]{2,1,0:T(8,128)(2,1)} %squeeze.59), channel_id=1, source_target_pairs={{0,8},{8,16},{16,24},{1,9},{9,17},{17,25},{2,10},{10,18},{18,26},{... | collective-permute-start | bytes 2654216 | tf_op jit(solution)/shard_map/ppermute | solution.py:57
  429.8 44.7 %collective-permute-start.15 = (bf16[3,384,384]{2,1,0:T(8,128)(2,1)}, bf16[3,384,384]{2,1,0:T(8,128)(2,1)}, u32[]{:S(2)}, u32[]{:S(2)}) collective-permute-start(bf16[3,384,384]{2,1,0:T(8,128)(2,1)} %squeeze.55), channel_id=1, source_target_pairs={{8,0},{16,8},{24,16},{9,1},{17,9},{25,17},{10,2},{18,10},{26,18},{... | collective-permute-start | bytes 2654216 | tf_op jit(solution)/shard_map/ppermute | solution.py:57
  438.7 35.8 %collective-permute-start.16 = (bf16[3,384,384]{2,1,0:T(8,128)(2,1)}, bf16[3,384,384]{2,1,0:T(8,128)(2,1)}, u32[]{:S(2)}, u32[]{:S(2)}) collective-permute-start(bf16[3,384,384]{2,1,0:T(8,128)(2,1)} %squeeze.56), channel_id=1, source_target_pairs={{0,8},{8,16},{16,24},{1,9},{9,17},{17,25},{2,10},{10,18},{18,26},{... | collective-permute-start | bytes 2654216 | tf_op jit(solution)/shard_map/ppermute | solution.py:57
  467.7 17.9 %collective-permute-start.21 = (bf16[384,384]{1,0:T(8,128)(2,1)}, bf16[384,384]{1,0:T(8,128)(2,1)S(1)}, u32[]{:S(2)}, u32[]{:S(2)}) collective-permute-start(bf16[384,384]{1,0:T(8,128)(2,1)} %get-tuple-element.262), channel_id=1, source_target_pairs={{4,0},{5,1},{6,2},{7,3},{12,8},{13,9},{14,10},{15,11},{20,16},{21,... | collective-permute-start | bytes 884744 | tf_op jit(solution)/shard_map/ppermute | solution.py:57
  469.0 16.6 %collective-permute-start.22 = (bf16[384,384]{1,0:T(8,128)(2,1)S(1)}, bf16[384,384]{1,0:T(8,128)(2,1)}, u32[]{:S(2)}, u32[]{:S(2)}) collective-permute-start(bf16[384,384]{1,0:T(8,128)(2,1)S(1)} %get-tuple-element.263), channel_id=1, source_target_pairs={{0,4},{1,5},{2,6},{3,7},{8,12},{9,13},{10,14},{11,15},{16,20},{17,... | collective-permute-start | bytes 884744 | tf_op jit(solution)/shard_map/ppermute | solution.py:57
  478.2 9.7 %collective-permute-start.17 = (bf16[384,384]{1,0:T(8,128)(2,1)}, bf16[384,384]{1,0:T(8,128)(2,1)S(1)}, u32[]{:S(2)}, u32[]{:S(2)}) collective-permute-start(bf16[384,384]{1,0:T(8,128)(2,1)} %get-tuple-element.264), channel_id=1, source_target_pairs={{4,0},{5,1},{6,2},{7,3},{12,8},{13,9},{14,10},{15,11},{20,16},{21,... | collective-permute-start | bytes 884744 | tf_op jit(solution)/shard_map/ppermute | solution.py:57
  479.5 9.4 %collective-permute-start.18 = (bf16[384,384]{1,0:T(8,128)(2,1)S(1)}, bf16[384,384]{1,0:T(8,128)(2,1)}, u32[]{:S(2)}, u32[]{:S(2)}) collective-permute-start(bf16[384,384]{1,0:T(8,128)(2,1)S(1)} %get-tuple-element.265), channel_id=1, source_target_pairs={{0,4},{1,5},{2,6},{3,7},{8,12},{9,13},{10,14},{11,15},{16,20},{17,... | collective-permute-start | bytes 884744 | tf_op jit(solution)/shard_map/ppermute | solution.py:57
  (25 other events, 358.7 us)
Sparse Core Ops, SparseCore 0:
  119.4 32.3 reduce-scatter.3
  290.8 31.2 reduce-scatter.5
  325.8 17.4 all-gather.7
Sparse Core Ops, SparseCore 1:
  122.2 78.7 all-gather.5
  203.3 77.7 all-gather.3
  349.8 72.5 reduce-scatter.7
